TPU v7x, 512 devices: a whole 4x8x8 slice. The times are simulated.
512 devices in a mesh: blk: 128 (over x, z_hi, y, core), grp: 4 (over z_lo).
Axes of the slice: x: 4, y: 8, z: 8 (z_hi: 2, z_lo: 4; z = z_hi * 4 + z_lo), core: 2. Of those that a mesh axis runs over, the one named last changes fastest.
Arguments:
- source_emb: float32 [128, 512, 400], P('blk', 'grp'), may hold values from -1.2 to 1.2
- source_state: float32 [128, 512], P('blk', 'grp'), may hold values from 0.01 to 0.1
- target_emb: float32 [128, 512, 400], P('blk', 'grp'), may hold values from -1.2 to 1.2
- target_state: float32 [128, 512], P('blk', 'grp'), may hold values from 0.01 to 0.1
- relation_emb: float32 [512, 400], replicated, may hold values from 0.1 to 1.9
- relation_state: float32 [512], replicated, may hold values from 0.01 to 0.1
- source_ids: int32 [2, 128, 4, 512], P(None, 'blk', 'grp'), may hold values from 0 to 127
- target_ids: int32 [2, 128, 4, 512], P(None, 'blk', 'grp'), may hold values from 0 to 127
- relation_ids: int32 [2, 128, 4, 512], P(None, 'blk', 'grp'), may hold values from 0 to 511
- edge_counts: int32 [2, 128, 4], P(None, 'blk', 'grp'), may hold values from 128 to 512, as said below
- sample_ids: int32 [2, 128, 4, 1, 256], P(None, 'blk', 'grp'), may hold values from 0 to 127
Outputs:
- source_out: float32 [128, 512, 400], P('blk', 'grp')
- source_state_out: float32 [128, 512], P('blk', 'grp')
- target_out: float32 [128, 512, 400], P('blk', 'grp')
- target_state_out: float32 [128, 512], P('blk', 'grp')
- relation_out: float32 [512, 400], replicated
- relation_state_out: float32 [512], replicated
Inputs may be any that keep to these rules, and one draw needn't show every extreme that they name: `edge_counts`: in every round some bucket is full.
All inputs are finite; a program needn't handle non-finite values.
Results may differ from a plain program's by a relative error of at most 0.0003.
Values sent between devices are 32-bit elements; how exact they have to be, the bound alone decides.
No kernel may reach another device: no remote copies, remote signals or barrier semaphores. Data moves between devices by JAX's collectives and lax.ppermute only.
A program may use at most 64 MiB of HBM per device.

v0:
```python
import jax
import jax.numpy as jnp
from jax import lax
from jax.sharding import PartitionSpec as P

learning_rate = 0.1
relation_rate = 0.1


def passed_along(block, axis, distance):
    devices = range(lax.axis_size(axis))
    route = [((i - distance) % len(devices), i) for i in devices]
    return lax.ppermute(block, axis, route)


def adagrad(weights, accum, grads, rate):
    fresh = accum + jnp.mean(grads * grads, axis=-1)
    return (weights - rate * grads * lax.rsqrt(fresh)[..., None], fresh)


def pick_rows(selector, table):
    return jnp.dot(selector, table, precision=lax.Precision.HIGHEST)


def put_rows(selector, values):
    return jnp.einsum("ir,id->rd", selector, values, precision=lax.Precision.HIGHEST)


def on_device(
    source_emb,
    source_state,
    target_emb,
    target_state,
    relation_emb,
    relation_state,
    source_ids,
    target_ids,
    relation_ids,
    edge_counts,
    sample_ids,
):
    source_rows = source_emb[0]
    source_acc = source_state[0]
    target_rows = target_emb[0]
    target_acc = target_state[0]
    rounds = source_ids.shape[0]
    slots = source_ids.shape[3]
    blocks = sample_ids.shape[3]
    samples = sample_ids.shape[4]
    per_block = slots // blocks
    slab_rows = source_rows.shape[0]
    kinds = relation_emb.shape[0]
    row_iota = jnp.arange(slab_rows, dtype=jnp.int32)
    total = jnp.zeros(relation_emb.shape, jnp.float32)
    for round_index in range(rounds):
        these_source = source_ids[round_index, 0, 0]
        these_target = target_ids[round_index, 0, 0]
        these_kinds = relation_ids[round_index, 0, 0]
        these_samples = sample_ids[round_index, 0, 0]
        live_count = edge_counts[round_index, 0, 0]
        held_source = source_rows
        held_target = target_rows

        def visit(block_index, running):
            grad_source, grad_target, grad_relation = running
            first = block_index * per_block
            picked_samples = lax.dynamic_index_in_dim(these_samples, block_index, 0, keepdims=False)
            alive = (first + jnp.arange(per_block, dtype=jnp.int32) < live_count).astype(
                jnp.float32
            )
            source_hot = (these_source[:, None] == row_iota[None, :]).astype(jnp.float32)
            target_hot = (these_target[:, None] == row_iota[None, :]).astype(jnp.float32)
            sample_hot = (picked_samples[:, None] == row_iota[None, :]).astype(jnp.float32)
            scale = relation_emb[these_kinds]
            left = pick_rows(source_hot, held_source)
            right = pick_rows(target_hot, held_target)
            sampled = pick_rows(sample_hot, held_target)
            query = left * scale
            positive = jnp.sum(query * right, axis=-1)
            negative = jnp.einsum("id,jd->ij", query, sampled, precision=lax.Precision.HIGHEST)
            pull = -alive * jax.nn.sigmoid(-positive)
            push = alive[:, None] * jax.nn.sigmoid(negative) / samples
            grad_query = pull[:, None] * right + jnp.dot(
                push, sampled, precision=lax.Precision.HIGHEST
            )
            grad_source = grad_source + put_rows(source_hot, grad_query * scale)
            to_samples = jnp.einsum("ij,id->jd", push, query, precision=lax.Precision.HIGHEST)
            grad_target = (
                grad_target
                + put_rows(target_hot, pull[:, None] * query)
                + put_rows(sample_hot, to_samples)
            )
            grad_relation = grad_relation + jax.ops.segment_sum(
                grad_query * left, these_kinds, num_segments=kinds
            )
            return (grad_source, grad_target, grad_relation)

        initial = (
            jnp.zeros_like(source_rows),
            jnp.zeros_like(target_rows),
            jnp.zeros(relation_emb.shape, jnp.float32),
        )
        grad_source, grad_target, grad_relation = lax.fori_loop(0, blocks, visit, initial)
        total = total + lax.psum(grad_relation, ("blk", "grp"))
        target_rows, target_acc = adagrad(target_rows, target_acc, grad_target, learning_rate)
        source_rows, source_acc = adagrad(source_rows, source_acc, grad_source, learning_rate)
        if round_index + 1 < rounds:
            source_rows, source_acc = passed_along((source_rows, source_acc), "blk", 1)
    relation_out, relation_state_out = adagrad(relation_emb, relation_state, total, relation_rate)
    return (
        source_rows[None],
        source_acc[None],
        target_rows[None],
        target_acc[None],
        relation_out,
        relation_state_out,
    )


def solution(mesh):
    in_specs = (
        P("blk", "grp", None),
        P("blk", "grp"),
        P("blk", "grp", None),
        P("blk", "grp"),
        P(),
        P(),
        P(None, "blk", "grp", None),
        P(None, "blk", "grp", None),
        P(None, "blk", "grp", None),
        P(None, "blk", "grp"),
        P(None, "blk", "grp", None, None),
    )
    out_specs = (
        P("blk", "grp", None),
        P("blk", "grp"),
        P("blk", "grp", None),
        P("blk", "grp"),
        P(),
        P(),
    )
    return jax.shard_map(
        on_device, mesh=mesh, in_specs=in_specs, out_specs=out_specs, check_vma=False
    )
```

profile of v0, /device:TPU:24, one launch (start us, length us, event | category | flops | bytes accessed | tf_op | source)
XLA Modules:
  0.0 351.3 jit_solution(18037519778036278335)
XLA Ops:
  7.2 0.7 fusion.49
  7.9 1.5 copy.23
  9.4 1.6 gather_fusion
  11.8 0.7 copy-done.8
  15.7 0.7 multiply_reduce_fusion.2
  16.4 0.7 divide_multiply_fusion.1
  17.0 1.9 fusion.8
  18.9 1.8 fusion.53
  22.5 0.7 bitcast_subtract_fusion.1
  23.2 1.9 collective-permute-start
  25.1 5.0 %collective-permute-start.1 = (f32[128]{0:T(128)}, f32[128]{0:T(128)}, u32[]{:S(2)}, u32[]{:S(2)}) collective-permute-start(f32[128]{0:T(128)} %get-tuple-element.92), channel_id=1, source_target_pairs={{508,0},{0,4},{4,8},{8,12},{12,16},{16,20},{20,24},{24,28},{28,32}... | collective-permute-start | bytes 1544 | tf_op jit(solution)/shard_map/ppermute | solution.py:13
  30.1 1.3 fusion.14
  31.4 1.8 fusion.55
  33.3 1.6 gather_fusion.1
  35.2 0.7 fusion.46
  35.9 2.5 copy.29
  39.0 0.7 copy-done.11
  39.7 4.7 %scatter_custom_fusion = f32[512,400]{1,0:T(8,128)S(1)} fusion(s32[512]{0:T(512)S(1)} %bitcast.81, f32[512,400]{1,0:T(8,128)} %copy.29, f32[]{:T(128)} %constant.39.clone.1), kind=kCustom, calls=%fused_computation.34 | custom fusion | flops 204800 | bytes 819712 | tf_op jit(solution)/shard_map/while/body/eval_jaxpr/scatter-add | solution.py:93
  44.9 1.5 fusion.25
  46.4 0.7 multiply_reduce_fusion.1
  48.4 1.9 fusion.9
  50.3 1.8 fusion.56
  52.1 1.8 fusion.54
  55.7 1.3 copy.30
  57.0 5.3 %scatter_custom_fusion.1 = f32[512,400]{1,0:T(8,128)} fusion(s32[512]{0:T(512)S(1)} %bitcast.80, f32[512,400]{1,0:T(8,128)} %copy.30, f32[]{:T(128)} %constant.39.clone.1), kind=kCustom, calls=%fused_computation.32 | custom fusion | flops 204800 | bytes 819712 | tf_op jit(solution)/shard_map/while/body/eval_jaxpr/scatter-add | solution.py:93
  62.3 2.5 add.156
  64.7 0.7 subtract_bitcast_fusion
  66.0 1.1 fusion.47
  67.1 1.6 subtract_bitcast_fusion.1
  68.7 272.3 %all-reduce.2.cloned.1.call-done = f32[512,400]{1,0:T(8,128)} async-done(((f32[512,400]{1,0:T(8,128)}), f32[512,400]{1,0:T(8,128)}) %all-reduce.2.cloned.1.call-update) | async-done | bytes 819216 | tf_op jit(solution)/shard_map/psum | solution.py:104
  341.0 1.5 multiply_reduce_fusion
  343.3 1.2 copy.32
  (54 shorter events, 11.5 us)
Async XLA Ops:
  7.2 333.8 %all-reduce.2.cloned.1.call-start = ((), (), s32[]{:S(2)}) async-start(), calls=%async_computation | async-start | bytes 2097152 | tf_op jit(solution)/shard_map/psum | solution.py:104
  7.9 1.5 copy-start.6
  11.1 0.7 copy-start.7
  11.1 3.3 copy-start.4
  11.8 0.7 copy-start.8
  12.4 0.7 copy-start.9
  14.4 0.9 copy-start.2
  21.4 0.7 copy-start.12
  23.2 21.6 %collective-permute-start = (f32[128,400]{0,1:T(8,128)}, f32[128,400]{0,1:T(8,128)}, u32[]{:S(2)}, u32[]{:S(2)}) collective-permute-start(f32[128,400]{0,1:T(8,128)} %bitcast_subtract_fusion.1), channel_id=1, source_target_pairs={{508,0},{0,4},{4,8},{8,12},{12,16},{16,20},{20,24},{24,28},{28,32}... | collective-permute-start | bytes 614408 | tf_op jit(solution)/shard_map/ppermute | solution.py:13
  25.1 40.8 %collective-permute-start.1 = (f32[128]{0:T(128)}, f32[128]{0:T(128)}, u32[]{:S(2)}, u32[]{:S(2)}) collective-permute-start(f32[128]{0:T(128)} %get-tuple-element.92), channel_id=1, source_target_pairs={{508,0},{0,4},{4,8},{8,12},{12,16},{16,20},{20,24},{24,28},{28,32}... | collective-permute-start | bytes 1544 | tf_op jit(solution)/shard_map/ppermute | solution.py:13
  35.9 2.5 copy-start.5
  38.4 1.3 copy-start.3
  39.0 0.7 copy-start.11
  54.5 1.1 copy-start.1
  68.7 273.8 %copy-start.10 = (f32[512]{0:T(512)S(1)}, f32[512]{0:T(512)}, u32[]{:S(2)}) copy-start(f32[512]{0:T(512)} %param.16) | copy-start | bytes 6148
  341.0 2.1 copy-start
Sparse Core Ops, SparseCore 0:
  64.9 276.0 all-reduce.1
where the time goes:
time: 352 us; the launch traced here: 351 us
  waiting for transfers between devices  272 us (77%)
  other arithmetic  22.6 us (6%)
  matrix products  19.7 us (6%)
  local copies, waits for them, and re-layouts  15.5 us (4%)
  between operations  14.3 us (4%)
  starting transfers between devices  6.93 us (2%)
    psum x1, waiting for transfers between devices, on_device(): total = total + lax.psum(grad_relation, ('blk', 'grp'))  272 us
    scatter-add x2, other arithmetic, visit(): jax.ops.segment_sum(grad_query * left, these_kinds, num_segments=kinds)  10 us
  transfers between devices with their start and end apart: 3, of which 1 were waited for; matrix products, arithmetic and copies ran while one was open for 11% of the time, Pallas kernels for 0%

commit v1 on v0

--- a/solution.py
+++ b/solution.py
@@ -101,7 +101,7 @@
             jnp.zeros(relation_emb.shape, jnp.float32),
         )
         grad_source, grad_target, grad_relation = lax.fori_loop(0, blocks, visit, initial)
-        total = total + lax.psum(grad_relation, ("blk", "grp"))
+        total = total + lax.psum(lax.psum(grad_relation, "blk"), "grp")
         target_rows, target_acc = adagrad(target_rows, target_acc, grad_target, learning_rate)
         source_rows, source_acc = adagrad(source_rows, source_acc, grad_source, learning_rate)
         if round_index + 1 < rounds:

time: 352 us -> 1700 us (4.83)
  the two profiles are of different devices: /device:TPU:24 before, /device:TPU:1 now
where the time goes in v1:
time: 1700 us
  waiting for transfers between devices  1620 us (95%)
  other arithmetic  22.2 us (1%)
  matrix products  21.5 us (1%)
    psum x2, waiting for transfers between devices, on_device(): total = total + lax.psum(lax.psum(grad_relation, 'blk'), 'grp')  1620 us
  transfers between devices with their start and end apart: 4, of which 2 were waited for; matrix products, arithmetic and copies ran while one was open for 2% of the time, Pallas kernels for 0%

profile of v1, /device:TPU:1, one launch (start us, length us, event | category | flops | bytes accessed | tf_op | source)
XLA Modules:
  0.0 1695.8 jit_solution(13688347112897573707)
XLA Ops:
  7.2 0.7 fusion.49
  7.9 1.5 copy.23
  9.4 1.6 gather_fusion
  11.8 0.7 copy-done.10
  15.7 0.7 multiply_reduce_fusion.2
  17.0 1.9 fusion.8
  18.9 1.8 fusion.53
  22.0 0.7 bitcast_subtract_fusion.1
  22.7 4.6 collective-permute-start
  27.3 2.1 collective-permute-start.1
  29.4 1.3 fusion.14
  30.7 1.8 fusion.55
  32.6 1.6 gather_fusion.1
  34.5 0.7 fusion.46
  35.2 2.6 copy.29
  38.4 0.7 copy-done.13
  39.1 5.2 scatter_custom_fusion
  44.8 1.5 fusion.25
  46.3 0.7 multiply_reduce_fusion.1
  47.6 1.9 fusion.9
  49.5 2.6 fusion.56
  52.1 1.8 fusion.54
  53.9 1.3 copy.30
  55.3 5.3 scatter_custom_fusion.1
  60.6 2.7 add.160
  64.0 1.7 multiply_reduce_fusion.3
  66.3 1548.6 %all-reduce.5.cloned.1.call-done = f32[512,400]{1,0:T(8,128)} async-done(((f32[512,400]{1,0:T(8,128)}), f32[512,400]{1,0:T(8,128)}) %all-reduce.5.cloned.1.call-update) | async-done | bytes 819216 | tf_op jit(solution)/shard_map/psum | solution.py:104
  1615.9 0.7 subtract_bitcast_fusion
  1616.6 1.6 subtract_bitcast_fusion.1
  1618.3 67.3 %all-reduce.3.cloned.1.call-done = f32[512,400]{1,0:T(8,128)} async-done(((f32[512,400]{1,0:T(8,128)}), f32[512,400]{1,0:T(8,128)}) %all-reduce.3.cloned.1.call-update) | async-done | bytes 819216 | tf_op jit(solution)/shard_map/psum | solution.py:104
  1685.5 1.5 multiply_reduce_fusion
  1687.8 1.2 copy.32
  (61 shorter events, 11.1 us)
Async XLA Ops:
  7.2 1607.7 %all-reduce.5.cloned.1.call-start = ((), (), s32[]{:S(2)}) async-start(), calls=%async_computation.1 | async-start | bytes 2097152 | tf_op jit(solution)/shard_map/psum | solution.py:104
  7.9 1.5 copy-start.8
  11.1 0.7 copy-start.9
  11.1 3.3 copy-start.6
  11.8 0.7 copy-start.10
  12.4 0.7 copy-start.11
  14.4 0.9 copy-start.4
  21.4 0.7 copy-start.14
  22.7 22.0 %collective-permute-start = (f32[128,400]{0,1:T(8,128)}, f32[128,400]{0,1:T(8,128)}, u32[]{:S(2)}, u32[]{:S(2)}) collective-permute-start(f32[128,400]{0,1:T(8,128)} %bitcast_subtract_fusion.1), channel_id=1, source_target_pairs={{508,0},{0,4},{4,8},{8,12},{12,16},{16,20},{20,24},{24,28},{28,32}... | collective-permute-start | bytes 614408 | tf_op jit(solution)/shard_map/ppermute | solution.py:13
  27.3 1587.6 %collective-permute-start.1 = (f32[128]{0:T(128)S(1)}, f32[128]{0:T(128)S(1)}, u32[]{:S(2)}, u32[]{:S(2)}) collective-permute-start(f32[128]{0:T(128)S(1)} %get-tuple-element.92), channel_id=1, source_target_pairs={{508,0},{0,4},{4,8},{8,12},{12,16},{16,20},{20,24},{24,28},{28,32}... | collective-permute-start | bytes 1544 | tf_op jit(solution)/shard_map/ppermute | solution.py:13
  35.2 2.6 copy-start.7
  37.7 1.3 copy-start.5
  38.4 0.7 copy-start.13
  39.1 7.2 copy-start.2
  63.3 2.4 copy-start.1
  63.3 1622.2 %all-reduce.3.cloned.1.call-start = ((), (), s32[]{:S(2)}) async-start(), calls=%async_computation | async-start | bytes 2097152 | tf_op jit(solution)/shard_map/psum | solution.py:104
  1614.9 1.1 copy-start.3
  1618.3 68.7 %copy-start.12 = (f32[512]{0:T(512)S(1)}, f32[512]{0:T(512)}, u32[]{:S(2)}) copy-start(f32[512]{0:T(512)} %param.16) | copy-start | bytes 6148
  1685.5 2.1 copy-start
Sparse Core Ops, SparseCore 0:
  63.4 1551.3 all-reduce.4
  1618.1 67.4 all-reduce.2
